TPU v7x, 32 devices: a whole 2x2x4 slice. The times are simulated.
32 devices in a mesh: groups: 2 (over y), row: 4 (over z), col: 2 (over x), rep: 2 (over core).
Axes of the slice: x: 2, y: 2, z: 4, core: 2. Of those that a mesh axis runs over, the one named last changes fastest.
Arguments:
- basis_values: bfloat16 [9216, 2048], P('row', ('col', 'rep')), may hold values from -6 to 6
- orbital_values: bfloat16 [4096, 128], P(('groups', 'col', 'rep')), parts along dimension 0, may hold values from -6 to 6
- z_tiles: bfloat16 [64, 128, 128], P('row'), may hold values from -0.00036621094 to 0.00036621094
- tile_pairs: int32 [64, 2], P('row'), may hold values from 0 to 15, as said below
Outputs:
- exchange: float32 [18432, 4, 2304], P(('groups', 'row'), ('col', 'rep')), parts along dimension 0
There are 2 independent parts, one for each index of `groups`. A program takes and returns all parts, laid end to end along the dimension named above; an argument that names none is the same for every part. Nothing has to cross between parts.
Inputs may be any that keep to these rules, and one draw needn't show every extreme that they name: `tile_pairs`: the column tile is the row tile plus 0 to 2, modulo 16; each tile is the row tile of exactly 4 pairs; a pair may repeat.
All inputs are finite; a program needn't handle non-finite values.
Results may differ from a plain program's by a relative error of at most 0.0075.
Values may be sent and summed in bfloat16 or wider, within the bound.
A program may use at most 192 MiB of HBM per device.

v0:
```python
import jax
import jax.numpy as jnp
from jax import lax
from jax.sharding import PartitionSpec as P


def mix_rows(rows, orbital_tiles, tile_block, pair_list):
    row_count = rows.shape[0]
    tile_count, tile_width, _ = orbital_tiles.shape
    row_tiles = rows.reshape(row_count, tile_count, tile_width)
    first_tile = pair_list[:, 0]
    second_tile = pair_list[:, 1]
    intersection = jnp.einsum(
        "npo,nqo->npq",
        orbital_tiles[first_tile],
        orbital_tiles[second_tile],
        preferred_element_type=jnp.float32,
    )
    weights = (tile_block.astype(jnp.float32) * intersection).astype(jnp.bfloat16)
    to_second = jnp.einsum(
        "rnp,npq->rnq",
        jnp.take(row_tiles, first_tile, axis=1),
        weights,
        preferred_element_type=jnp.float32,
    )
    to_first = jnp.einsum(
        "rnq,npq->rnp",
        jnp.take(row_tiles, second_tile, axis=1),
        weights,
        preferred_element_type=jnp.float32,
    )
    labels = jnp.arange(tile_count, dtype=jnp.int32)
    hit_first = (first_tile[:, None] == labels[None, :]).astype(jnp.float32)
    hit_second = (second_tile[:, None] == labels[None, :]).astype(jnp.float32)
    return jnp.einsum("rnq,nt->rtq", to_second, hit_second) + jnp.einsum(
        "rnp,nt->rtp", to_first, hit_first
    )


def on_device(basis_values, orbital_values, z_tiles, tile_pairs):
    groups = lax.axis_size(("col", "rep"))
    block_rows, block_points = basis_values.shape
    slice_count = block_rows // groups
    orbitals = lax.all_gather(orbital_values, ("col", "rep"), axis=0, tiled=True)
    points = orbitals.shape[0]
    tile_width = z_tiles.shape[1]
    orbital_tiles = orbitals.reshape(points // tile_width, tile_width, orbitals.shape[1])
    gathered = lax.all_gather(basis_values, "row", axis=0, tiled=True)
    shaped = gathered.reshape(-1, groups, slice_count, block_points)
    received = lax.all_to_all(shaped, ("col", "rep"), split_axis=1, concat_axis=3, tiled=True)
    columns = received.reshape(-1, points)
    own_slice = lax.dynamic_slice_in_dim(
        columns, lax.axis_index("row") * slice_count, slice_count, 0
    )
    zero_mix = jnp.zeros((own_slice.shape[0], points // tile_width, tile_width), jnp.float32)
    running = zero_mix + mix_rows(
        own_slice,
        orbital_tiles,
        lax.all_gather(z_tiles, "row", axis=0, tiled=True),
        lax.all_gather(tile_pairs, "row", axis=0, tiled=True),
    )
    mixed_half = running.reshape(own_slice.shape[0], points).astype(jnp.bfloat16)
    mixed_half = lax.all_gather(mixed_half, ("col", "rep"), axis=0, tiled=True)
    product = lax.dot_general(
        mixed_half, columns, (((1,), (1,)), ((), ())), preferred_element_type=jnp.float32
    )
    return product.reshape(block_rows, 1, -1)


def solution(mesh):
    placed = (
        P("row", ("col", "rep")),
        P(("groups", "col", "rep"), None),
        P("row", None, None),
        P("row", None),
    )
    return jax.shard_map(
        on_device,
        mesh=mesh,
        in_specs=placed,
        out_specs=P(("groups", "row"), ("col", "rep"), None),
        check_vma=False,
    )
```

profile of v0, /device:TPU:0, one launch (start us, length us, event | category | flops | bytes accessed | tf_op | source)
XLA Modules:
  0.0 527.8 jit_solution(7874156168469878912)
XLA Ops:
  6.5 0.7 all-gather.7.cloned.1.call-update
  7.3 171.2 %all-gather.7.cloned.1.call-done = bf16[9216,512]{1,0:T(8,128)(2,1)} async-done(((bf16[2304,512]{1,0:T(8,128)(2,1)}), bf16[9216,512]{1,0:T(8,128)(2,1)}) %all-gather.7.cloned.1.call-update) | async-done | bytes 9437200 | tf_op jit(solution)/shard_map/all_gather | solution.py:48
  178.4 8.3 %copy.25 = bf16[4,4,576,512]{3,2,0,1:T(8,128)(2,1)} copy(bf16[4,4,576,512]{3,2,1,0:T(8,128)(2,1)} %bitcast.70) | data formatting | bytes 18874368 | tf_op jit(solution)/shard_map/reshape | solution.py:49
  186.7 6.0 %all-to-all-start = ((bf16[4,4,576,512]{3,2,0,1:T(8,128)(2,1)}), bf16[4,4,576,512]{3,2,0,1:T(8,128)(2,1)}, u32[]{:S(2)}, u32[]{:S(2)}) async-start(bf16[4,4,576,512]{3,2,0,1:T(8,128)(2,1)} %copy.25), calls=%async_computation | async-start | bytes 18874368 | tf_op jit(solution)/shard_map/all_to_all | solution.py:50
  192.7 0.7 all-gather.5.cloned.1.call-update
  193.5 7.9 %all-gather = s32[4,16,2]{1,2,0:T(2,128)S(1)} all-gather(s32[1,16,2]{1,2,0:T(2,128)S(1)} %bitcast.72), channel_id=1, replica_groups=mesh['groups'=2,'row'=4,'col'=2,'rep'=2] {'row'}, dimensions={0}, use_global_device_ids=true | all-gather | bytes 640 | tf_op jit(solution)/shard_map/all_gather | solution.py:60
  201.3 0.1 reshape.63
  201.5 99.2 %all_gather.17 = bf16[2048,128]{1,0:T(8,128)(2,1)S(1)} all-gather(bf16[512,128]{1,0:T(8,128)(2,1)S(1)} %copy-done), channel_id=1, replica_groups=mesh['groups'=2,'row'=4,'col'=2,'rep'=2] {'col','rep'}, dimensions={0}, use_global_device_ids=true | all-gather | bytes 655360 | tf_op jit(solution)/shard_map/all_gather | solution.py:44
  300.6 0.9 gather_fusion.1
  301.6 2.1 gather_fusion
  303.8 5.1 multiply_convert_fusion
  308.9 12.2 %copy.26 = bf16[4,1,576,4,512]{4,3,2,0,1:T(4,128)(2,1)} copy(bf16[4,1,576,4,512]{4,2,0,3,1:T(8,128)(2,1)} %bitcast.9) | data formatting | bytes 18874368 | tf_op jit(solution)/shard_map/all_to_all | solution.py:50
  321.1 11.4 %copy.33 = bf16[288,8,4,512]{3,1,2,0:T(8,128)(2,1)} copy(bf16[288,8,4,512]{3,2,1,0:T(4,128)(2,1)} %bitcast.66) | data formatting | bytes 18874368
  332.5 2.3 copy_bitcast_fusion.1
  334.8 6.2 %gather_fusion.3 = bf16[64,576,128]{2,1,0:T(8,128)(2,1)} fusion(bf16[576,16,128]{2,0,1:T(8,128)(2,1)S(1)} %copy_bitcast_fusion.1, s32[1024]{0:T(1024)S(1)} %get-tuple-element.18), kind=kCustom, calls=%fused_computation.1.clone | custom fusion | bytes 18874624 | tf_op jit(solution)/shard_map/jit(_take)/gather | solution.py:28
  341.0 6.1 %gather_fusion.2 = bf16[64,576,128]{2,1,0:T(8,128)(2,1)} fusion(bf16[576,16,128]{2,0,1:T(8,128)(2,1)S(1)} %copy_bitcast_fusion.1, s32[1024]{0:T(1024)S(1)} %get-tuple-element.19), kind=kCustom, calls=%fused_computation.clone | custom fusion | bytes 18874624 | tf_op jit(solution)/shard_map/jit(_take)/gather | solution.py:22
  347.1 6.1 %fusion.15 = bf16[576,64,128]{2,0,1:T(8,128)(2,1)S(1)} fusion(bf16[64,128,128]{2,1,0:T(8,128)(2,1)} %multiply_convert_fusion, bf16[64,576,128]{2,1,0:T(8,128)(2,1)} %gather_fusion.3, pred[64]{0:T(512)(128)(4,1)S(1)} %get-tuple-element.14), kind=kOutput, calls=%fused_computation.18 | convolution fusion | flops 1212678144 | bytes 20971584 | tf_op jit(solution)/shard_map/rnq,npq->rnp/dot_general | solution.py:26
  353.2 5.2 fusion
  358.4 6.0 %fusion.12 = bf16[576,64,128]{2,0,1:T(8,128)(2,1)S(1)} fusion(bf16[64,128,128]{2,1,0:T(8,128)(2,1)} %multiply_convert_fusion, bf16[64,576,128]{2,1,0:T(8,128)(2,1)} %gather_fusion.2, pred[64]{0:T(512)(128)(4,1)S(1)} %get-tuple-element.6), kind=kOutput, calls=%fused_computation.17 | convolution fusion | flops 1212678144 | bytes 20971584 | tf_op jit(solution)/shard_map/rnp,npq->rnq/dot_general | solution.py:20
  364.3 20.1 %add_convert_fusion = bf16[16,576,128]{2,0,1:T(8,128)(2,1)S(1)} fusion(f32[16,576,128]{2,0,1:T(8,128)S(1)} %fusion, bf16[576,64,128]{2,0,1:T(8,128)(2,1)S(1)} %fusion.12, s32[64]{0:T(128)S(1)} %get-tuple-element.10), kind=kOutput, calls=%fused_computation.21 | convolution fusion | flops 153355264 | bytes 16515328 | tf_op jit(solution)/shard_map/rnq,nt->rtq/dot_general | solution.py:35
  384.5 2.0 copy.43
  386.5 61.7 %all-gather.9.cloned.1.call-done = bf16[2304,2048]{1,0:T(8,128)(2,1)} async-done(((bf16[576,2048]{1,0:T(8,128)(2,1)}), bf16[2304,2048]{1,0:T(8,128)(2,1)}) %all-gather.9.cloned.1.call-update) | async-done | bytes 9437200 | tf_op jit(solution)/shard_map/all_gather | solution.py:63
  448.2 29.7 %convolution_bitcast_fusion = f32[2304,1,2304]{2,0,1:T(8,128)} fusion(bf16[2304,2048]{1,0:T(8,128)(2,1)} %all-gather.9.cloned.1.call-done, bf16[2304,2048]{1,0:T(8,128)(2,1)} %bitcast.68), kind=kOutput, calls=%fused_computation.4 | convolution fusion | flops 21743271936 | bytes 40108032 | tf_op jit(solution)/shard_map/dot_general | solution.py:64
  477.9 42.9 %copy.31 = f32[2304,1,2304]{2,1,0:T(1,128)} copy(f32[2304,1,2304]{2,0,1:T(8,128)} %convolution_bitcast_fusion) | data formatting | bytes 42467328 | tf_op jit(solution)/shard_map/reshape | solution.py:67
  (15 shorter events, 0.2 us)
Async XLA Ops:
  6.5 171.9 %all-gather.7.cloned.1.call-start = ((), (), s32[]{:S(2)}) async-start(), calls=%async_computation.2 | async-start | bytes 11796480 | tf_op jit(solution)/shard_map/all_gather | solution.py:48
  186.7 6.8 %copy-start.1 = (s32[16,2]{0,1:T(2,128)S(1)}, s32[16,2]{0,1:T(2,128)}, u32[]{:S(2)}) copy-start(s32[16,2]{0,1:T(2,128)} %param.9) | copy-start | bytes 388
  186.7 14.8 %copy-start = (bf16[512,128]{1,0:T(8,128)(2,1)S(1)}, bf16[512,128]{1,0:T(8,128)(2,1)}, u32[]{:S(2)}) copy-start(bf16[512,128]{1,0:T(8,128)(2,1)} %param.7) | copy-start | bytes 393220
  186.7 122.2 %all-to-all-start = ((bf16[4,4,576,512]{3,2,0,1:T(8,128)(2,1)}), bf16[4,4,576,512]{3,2,0,1:T(8,128)(2,1)}, u32[]{:S(2)}, u32[]{:S(2)}) async-start(bf16[4,4,576,512]{3,2,0,1:T(8,128)(2,1)} %copy.25), calls=%async_computation | async-start | bytes 18874368 | tf_op jit(solution)/shard_map/all_to_all | solution.py:50
  192.7 111.1 %all-gather.5.cloned.1.call-start = ((), (), s32[]{:S(2)}) async-start(), calls=%async_computation.1 | async-start | bytes 2621440 | tf_op jit(solution)/shard_map/all_gather | solution.py:59
  193.4 254.8 %all-gather.9.cloned.1.call-start = ((), (), s32[]{:S(2)}) async-start(), calls=%async_computation.3 | async-start | bytes 11796480 | tf_op jit(solution)/shard_map/all_gather | solution.py:63
Sparse Core Ops, SparseCore 0:
  8.9 169.4 all-gather.6
  195.1 44.6 all-gather.4
  386.6 61.5 all-gather.8
where the time goes:
time: 537 us; the launch traced here: 528 us
  waiting for transfers between devices  234 us (44%)
  blocking collectives  107 us (20%)
  local copies, waits for them, and re-layouts  94.6 us (18%)
  matrix products  72.1 us (13%)
  between operations  13.6 us (3%)
  starting transfers between devices  6.05 us (1%)
    all_gather x1, waiting for transfers between devices, on_device(): gathered = lax.all_gather(basis_values, 'row', axis=0, tiled=True)  171 us
    all_gather x1, blocking collectives, on_device(): lax.all_gather(orbital_values, ('col', 'rep'), axis=0, tiled=True)  99.2 us
    all_gather x1, waiting for transfers between devices, on_device(): mixed_half = lax.all_gather(mixed_half, ('col', 'rep'), axis=0, tiled=True)  61.7 us
    reshape x1, local copies, waits for them, and re-layouts, on_device(): return product.reshape(block_rows, 1, -1)  42.9 us
    dot_general x1, matrix products, on_device(): lax.dot_general(mixed_half, columns, (((1,), (1,)), ((), ())), preferred_...  29.7 us
    dot_general x1, matrix products, mix_rows(): jnp.einsum('rnq,nt->rtq', to_second, hit_second)  20.1 us
    unnamed x7, local copies, waits for them, and re-layouts  13.5 us
    all_to_all x1, local copies, waits for them, and re-layouts, on_device(): lax.all_to_all(shaped, ('col', 'rep'), split_axis=1, concat_axis=3, tiled...  12.2 us
  transfers between devices with their start and end apart: 4, of which 2 were waited for; matrix products, arithmetic and copies ran while one was open for 2% of the time, Pallas kernels for 0%

commit v1 on v0

v1 whole, which is shorter than its diff:
```python
import functools

import jax
import jax.numpy as jnp
from jax import lax
from jax.experimental import pallas as pl
from jax.experimental.pallas import tpu as pltpu
from jax.sharding import PartitionSpec as P

MESH = pl.DeviceIdType.MESH
BAND = 3


def gather_kernel(dims, basis, orb, z, pairs, a_all, cols, orb_all, z_all, pairs_all,
                  loc_sem, xs_sem, xr_sem, os_sem, or_sem, zs_sem, zo_sem, zr_sem,
                  ys_sem, yr_sem, ts_sem, to_sem, tr_sem, ps_sem, po_sem, pr_sem,
                  ds_sem, dr_sem):
    G, R, X, K = dims
    C = X * K
    width = basis.shape[2]
    half = width // G
    n_pair = z.shape[0]
    part = z.shape[1] // C
    g = lax.axis_index("groups")
    r = lax.axis_index("row")
    x = lax.axis_index("col")
    k = lax.axis_index("rep")
    c = x * K + k

    def col_of(dx, dk):
        return lax.rem(x + dx, X) * K + lax.rem(k + dk, K)

    def dev(dg=0, row=None, dx=0, dk=0):
        return (lax.rem(g + dg, G), r if row is None else row, lax.rem(x + dx, X), lax.rem(k + dk, K))

    def remote(src, dst, send, recv, device):
        return pltpu.make_async_remote_copy(src_ref=src, dst_ref=dst, send_sem=send, recv_sem=recv,
                                            device_id=device, device_id_type=MESH)

    others = [(dx, dk) for dx in range(X) for dk in range(K) if dx or dk]
    barrier = pltpu.get_barrier_semaphore()
    for dx, dk in others:
        pl.semaphore_signal(barrier, inc=1, device_id=dev(dx=dx, dk=dk), device_id_type=MESH)
    for dr in (1, R - 1):
        pl.semaphore_signal(barrier, inc=1, device_id=dev(row=lax.rem(r + dr, R)), device_id_type=MESH)
    for dg in range(1, G):
        pl.semaphore_signal(barrier, inc=1, device_id=dev(dg=dg), device_id_type=MESH)
    pl.semaphore_wait(barrier, len(others) + 2 + G - 1)

    def lanes(point_block):
        return pl.ds(pl.multiple_of(point_block * width, 128), width)

    def half_lanes(point_block, group):
        return pl.ds(pl.multiple_of(point_block * width + group * half, 128), half)

    def tile_rows(block):
        return z_all.at[pl.ds(block * n_pair, n_pair), pl.ds(pl.multiple_of(c * part, 16), part), :]

    own_rows = z.at[:, pl.ds(pl.multiple_of(c * part, 16), part), :]

    def up():
        return dev(row=r + 1)

    def down():
        return dev(row=r - 1)

    def own_tiles(way, to):
        return (remote(own_rows, tile_rows(r), to_sem.at[way], tr_sem.at[r], to),
                remote(pairs, pairs_all.at[r], po_sem.at[way], pr_sem.at[r], to))

    def pass_tiles(block, to):
        return (remote(tile_rows(block), tile_rows(block), ts_sem.at[block], tr_sem.at[block], to),
                remote(pairs_all.at[block], pairs_all.at[block], ps_sem.at[block], pr_sem.at[block], to))

    def piece(block, point_block, group):
        return cols.at[block, :, half_lanes(point_block, group)]

    def own_piece(point_block, way, to, local):
        if local:
            src = basis.at[c, :, pl.ds(pl.multiple_of(g * half, 128), half)]
        else:
            src = a_all.at[c, :, half_lanes(point_block, g)]
        return remote(src, piece(r, point_block, g), zo_sem.at[way, point_block],
                      zr_sem.at[r, point_block], to)

    def pass_piece(block, point_block, to):
        ref = piece(block, point_block, g)
        return remote(ref, ref, zs_sem.at[block, point_block], zr_sem.at[block, point_block], to)

    def swap_piece(block, point_block, dg):
        ref = piece(block, point_block, g)
        return remote(ref, ref, ys_sem.at[dg - 1, block, point_block],
                      yr_sem.at[dg - 1, block, point_block], dev(dg=dg))

    def got_piece(block, point_block, dg):
        ref = piece(block, point_block, lax.rem(g + G - dg, G))
        return remote(ref, ref, ys_sem.at[dg - 1, block, point_block],
                      yr_sem.at[dg - 1, block, point_block], dev(dg=dg))

    def each(action, items):
        for item in items:
            getattr(item, action)()

    def both_ways(do):
        pl.when(r + 1 < R)(lambda: do(0, up()))
        pl.when(r > 0)(lambda: do(1, down()))

    def start_own(point_block, local=False):
        both_ways(lambda way, to: own_piece(point_block, way, to, local).start())

    both_ways(lambda way, to: each("start", own_tiles(way, to)))
    start_own(c, True)

    def to_core(dk, s):
        ref = a_all.at[s, :, lanes(c)]
        return remote(basis.at[s], ref, xs_sem.at[0, dk, s], xr_sem.at[0, dk, s], dev(dk=K - dk))

    def to_chip(dx, s):
        ref = a_all.at[s, :, lanes(c)]
        return remote(basis.at[s], ref, xs_sem.at[dx, 0, s], xr_sem.at[dx, 0, s], dev(dx=X - dx))

    def from_other(dx, dk, s):
        ref = a_all.at[s, :, lanes(col_of(dx, dk))]
        return remote(ref, ref, xs_sem.at[dx, dk, s], xr_sem.at[dx, dk, s], dev(dk=1))

    def hand_on(dx, dk, s):
        ref = a_all.at[s, :, lanes(col_of(dx, 0))]
        return remote(ref, ref, xs_sem.at[dx, dk, s], xr_sem.at[dx, dk, s], dev(dk=K - dk))

    own_orb = orb_all.at[pl.ds(pl.multiple_of(c * width, 16), width), :]

    def orb_to(dx, dk):
        return remote(orb, own_orb, os_sem.at[dx, dk], or_sem.at[dx, dk], dev(dx=lax.rem(X - dx, X), dk=lax.rem(K - dk, K)))

    def orb_from(dx, dk):
        ref = orb_all.at[pl.ds(pl.multiple_of(col_of(dx, dk) * width, 16), width), :]
        return remote(ref, ref, os_sem.at[dx, dk], or_sem.at[dx, dk], dev(dk=1))

    order = [(dx, dk) for dx in range(X) for dk in range(K)]
    for ex, ek in order:
        for dk in range(1, K):
            to_core(dk, lax.rem(x + ex, X) * K + lax.rem(k + K - dk + ek, K)).start()
        for dx in range(1, X):
            to_chip(dx, lax.rem(x + X - dx + ex, X) * K + lax.rem(k + ek, K)).start()
        if ex == 0 and ek == 0:
            for dx, dk in others:
                orb_to(dx, dk).start()

    local = [
        pltpu.make_async_copy(basis, a_all.at[:, :, lanes(c)], loc_sem.at[0]),
        pltpu.make_async_copy(orb, own_orb, loc_sem.at[1]),
        pltpu.make_async_copy(own_rows, tile_rows(r), loc_sem.at[2]),
        pltpu.make_async_copy(pairs, pairs_all.at[r], loc_sem.at[3]),
    ]
    for copy in local:
        copy.start()

    for dk in range(1, K):
        from_other(0, dk, c).wait_recv()
        start_own(col_of(0, dk))

    def each_block(step, below, above):
        pl.when(r - step >= 0)(lambda: below(r - step))
        pl.when(r + step < R)(lambda: above(r + step))

    def relay_tiles(step, carry):
        def take(block, last, to):
            for t in pass_tiles(block, to):
                t.wait_recv()

            @pl.when(last)
            def _():
                for t in pass_tiles(block, to):
                    t.start()

        each_block(step, lambda b: take(b, r + 1 < R, up()), lambda b: take(b, r > 0, down()))
        return carry

    def relay(step, dxs):
        def take(block, point_block, more, to):
            pass_piece(block, point_block, to).wait_recv()
            pl.when(more)(lambda: pass_piece(block, point_block, to).start())
            for dg in range(1, G):
                swap_piece(block, point_block, dg).start()

        for dx in dxs:
            for dk in range(K):
                p = col_of(dx, dk)
                each_block(step, lambda b: take(b, p, r + 1 < R, up()), lambda b: take(b, p, r > 0, down()))

    lax.fori_loop(1, R, relay_tiles, 0)
    for copy in local[2:]:
        copy.wait()

    def all_rows(col):
        return z_all.at[:, pl.ds(pl.multiple_of(col * part, 16), part), :]

    def spread(dx, dk):
        return remote(all_rows(c), all_rows(c), ds_sem.at[dx, dk], dr_sem.at[dx, dk],
                      dev(dx=lax.rem(X - dx, X), dk=lax.rem(K - dk, K)))

    def spread_in(dx, dk):
        ref = all_rows(col_of(dx, dk))
        return remote(ref, ref, ds_sem.at[dx, dk], dr_sem.at[dx, dk], dev(dk=1))

    for dx, dk in others:
        spread(dx, dk).start()

    relay(1, [0])
    for dx in range(1, X):
        from_other(dx, 0, c).wait_recv()
        start_own(col_of(dx, 0))
    for dx in range(1, X):
        for dk in range(1, K):
            s = col_of(0, K - dk)
            from_other(dx, 0, s).wait_recv()
            hand_on(dx, dk, s).start()
    for dx in range(1, X):
        for dk in range(1, K):
            from_other(dx, dk, c).wait_recv()
            start_own(col_of(dx, dk))

    def first_part(step, carry):
        relay(step, [0])
        return carry

    def second_part(step, carry):
        relay(step, list(range(1, X)))
        return carry

    lax.fori_loop(2, R, first_part, 0)
    relay(1, list(range(1, X)))

    for dx in range(1, X):
        for ex, ek in order:
            if ex == 0 and ek < 1:
                for dk in range(1, K):
                    hand_on(dx, dk, c).start()
            elif ex:
                s = col_of(ex, ek)
                from_other(dx, 0, s).wait_recv()
                for dk in range(1, K):
                    hand_on(dx, dk, s).start()
            else:
                s = col_of(0, ek)
                for dk in range(1, K):
                    if K - dk != ek:
                        hand_on(dx, dk, s).start()

    lax.fori_loop(2, R, second_part, 0)

    for dx, dk in others:
        for ex, ek in order:
            if ex == 0 and ek == 0:
                continue
            if dk == 0 and dx:
                continue
            from_other(dx, dk, col_of(ex, ek)).wait_recv()
        orb_from(dx, dk).wait_recv()
        spread_in(dx, dk).wait_recv()
    local[0].wait()
    local[1].wait()
    own = pltpu.make_async_copy(a_all.at[c], cols.at[r], loc_sem.at[4])
    own.start()

    def finish(block, carry):
        @pl.when(block != r)
        def _():
            def one(p, inner):
                for dg in range(1, G):
                    got_piece(block, p, dg).wait_recv()
                    swap_piece(block, p, dg).wait_send()
                pl.when(jnp.logical_and(block < r, r + 1 < R))(lambda: pass_piece(block, p, up()).wait_send())
                pl.when(jnp.logical_and(block > r, r > 0))(lambda: pass_piece(block, p, down()).wait_send())
                return inner

            lax.fori_loop(0, C, one, 0)
            pl.when(jnp.logical_and(block < r, r + 1 < R))(lambda: each("wait_send", pass_tiles(block, up())))
            pl.when(jnp.logical_and(block > r, r > 0))(lambda: each("wait_send", pass_tiles(block, down())))
        return carry

    lax.fori_loop(0, R, finish, 0)
    both_ways(lambda way, to: each("wait_send", own_tiles(way, to)))
    for dx, dk in order:
        both_ways(lambda way, to: own_piece(col_of(dx, dk), way, to, False).wait_send())
    for dx, dk in others:
        for ex, ek in order:
            s = col_of(ex, ek)
            from_other(dx, dk, s).wait_send()
        orb_to(dx, dk).wait_send()
        spread(dx, dk).wait_send()
    own.wait()


def product_kernel(pairs, orb, z, a, b, out, metric, upper, mixed):
    tiles = orb.shape[0] // 128
    n_local = z.shape[0] // pairs.shape[0]

    @pl.when(pl.program_id(0) == 0)
    def _():
        upper[...] = jnp.zeros_like(upper)

        def one(i, carry):
            block = i // n_local
            at = (i - block * n_local) * 2
            first = pairs[block, 0, at]
            second = pairs[block, 0, at + 1]
            offset = lax.rem(second - first + tiles, tiles)
            rows = orb[pl.ds(pl.multiple_of(first * 128, 128), 128), :]
            columns = orb[pl.ds(pl.multiple_of(second * 128, 128), 128), :]
            inter = lax.dot_general(rows, columns, (((1,), (1,)), ((), ())), preferred_element_type=jnp.float32)
            weight = (z[i].astype(jnp.float32) * inter).astype(jnp.bfloat16).astype(jnp.float32)
            slot = first * BAND + offset
            upper[slot] = upper[slot] + weight
            return carry

        lax.fori_loop(0, z.shape[0], one, 0, unroll=4)
        metric[...] = jnp.zeros_like(metric)
        for t in range(tiles):
            for offset in range(BAND):
                value = upper[t * BAND + offset]
                turned = value.T
                u = (t + offset) % tiles
                here, there = slice(t * 128, t * 128 + 128), slice(u * 128, u * 128 + 128)
                if offset == 0:
                    metric[here, here] = (value + turned).astype(jnp.bfloat16)
                else:
                    metric[here, there] = value.astype(jnp.bfloat16)
                    metric[there, here] = turned.astype(jnp.bfloat16)

    for u in range(0, tiles, 2):
        span = [(u - BAND + 1 + m) % tiles for m in range(2 * BAND)]
        runs = []
        for t in span:
            if runs and runs[-1][1] == t:
                runs[-1][1] = t + 1
            else:
                runs.append([t, t + 1])
        total = None
        for lo, hi in runs:
            term = jnp.dot(a[:, lo * 128:hi * 128], metric[lo * 128:hi * 128, u * 128:u * 128 + 256],
                           preferred_element_type=jnp.float32)
            total = term if total is None else total + term
        mixed[:, u * 128:u * 128 + 256] = total.astype(jnp.bfloat16)

    rows = a.shape[0]
    lines = b.shape[0] // 128
    step = next(s for s in (3, 2, 1) if lines % s == 0)

    for i in range(lines // step):
        value = lax.dot_general(mixed[...], b[i * step * 128:(i + 1) * step * 128, :],
                                (((1,), (1,)), ((), ())), preferred_element_type=jnp.float32)
        for q in range(step):
            out[pl.ds(i * step + q, rows, stride=lines), :] = value[:, q * 128:q * 128 + 128]


def on_device(dims, basis_values, orbital_values, z_tiles, tile_pairs):
    G, R, X, K = dims
    C = X * K
    block_rows, width = basis_values.shape
    S = block_rows // C
    points = width * C
    n_pair, tile, _ = z_tiles.shape
    orbs = orbital_values.shape[1]
    flat = tile_pairs.reshape(1, 2 * n_pair)
    flat = jnp.pad(flat, ((0, 7), (0, 128 - 2 * n_pair)))
    bf16 = jnp.bfloat16
    any_spec = pl.BlockSpec(memory_space=pl.ANY)
    dma = pltpu.SemaphoreType.DMA
    a_all, cols, orb_all, z_all, pairs_all = pl.pallas_call(
        functools.partial(gather_kernel, dims),
        out_shape=[
            jax.ShapeDtypeStruct((C, S, points), bf16),
            jax.ShapeDtypeStruct((R, S, points), bf16),
            jax.ShapeDtypeStruct((points, orbs), bf16),
            jax.ShapeDtypeStruct((R * n_pair, tile, tile), bf16),
            jax.ShapeDtypeStruct((R, 8, 128), jnp.int32),
        ],
        in_specs=[any_spec] * 4,
        out_specs=[any_spec] * 5,
        scratch_shapes=[
            dma((5,)), dma((X, K, C)), dma((X, K, C)), dma((X, K)), dma((X, K)),
            dma((R, C)), dma((2, C)), dma((R, C)),
            dma((G - 1, R, C)), dma((G - 1, R, C)),
            dma((R,)), dma((2,)), dma((R,)), dma((R,)), dma((2,)), dma((R,)),
            dma((X, K)), dma((X, K)),
        ],
        compiler_params=pltpu.CompilerParams(collective_id=0, has_side_effects=True),
    )(basis_values.reshape(C, S, width), orbital_values, z_tiles, flat)

    a = a_all.reshape(C * S, points)
    b = cols.reshape(R * S, points)
    lines = R * S // 128
    rows = next(m for m in range(384, 0, -16) if block_rows % m == 0)
    once = pl.Buffered(1)

    def whole(shape):
        return pl.BlockSpec(shape, lambda i: (0,) * len(shape), pipeline_mode=once)

    product = pl.pallas_call(
        product_kernel,
        grid=(block_rows // rows,),
        out_shape=jax.ShapeDtypeStruct((block_rows * lines, 128), jnp.float32),
        in_specs=[
            pl.BlockSpec(memory_space=pltpu.SMEM),
            whole((points, orbs)),
            whole((R * n_pair, tile, tile)),
            pl.BlockSpec((rows, points), lambda i: (i, 0)),
            whole((R * S, points)),
        ],
        out_specs=pl.BlockSpec((rows * lines, 128), lambda i: (i, 0)),
        scratch_shapes=[
            pltpu.VMEM((points, points), bf16),
            pltpu.VMEM((points // 128 * BAND, tile, tile), jnp.float32),
            pltpu.VMEM((rows, points), bf16),
        ],
        compiler_params=pltpu.CompilerParams(vmem_limit_bytes=56 * 1024 * 1024),
    )(pairs_all, orb_all, z_all, a, b)
    return product.reshape(block_rows, 1, R * S)


def solution(mesh):
    dims = tuple(mesh.shape[name] for name in ("groups", "row", "col", "rep"))
    placed = (
        P("row", ("col", "rep")),
        P(("groups", "col", "rep"), None),
        P("row", None, None),
        P("row", None),
    )
    return jax.shard_map(
        functools.partial(on_device, dims),
        mesh=mesh,
        in_specs=placed,
        out_specs=P(("groups", "row"), ("col", "rep"), None),
        check_vma=False,
    )
```

time: 537 us -> 274 us (0.51); the launches traced: 528 us -> 274 us
  Pallas kernels: 0 us -> 273 us
  waiting for transfers between devices: 234 us -> 0 us
  blocking collectives: 107 us -> 0 us
  local copies, waits for them, and re-layouts: 94.6 us -> 1.44 us
  matrix products: 72.1 us -> 0 us
  between operations: 13.6 us -> 0.01 us
  starting transfers between devices: 6.05 us -> 0 us
    pallas_call x0 -> x2, Pallas kernels: none -> 273 us  [the longest x1 224 us: on_device(): pl.pallas_call(functools.partial(gather_kernel, dims), out_shape=[jax.Sha...]
    all_gather x3 -> x0, waiting for transfers between devices: 233 us -> none  [the longest x1 171 us: on_device(): gathered = lax.all_gather(basis_values, 'row', axis=0, tiled=True)]
    all_gather x2 -> x0, blocking collectives: 107 us -> none  [the longest x1 99.2 us: on_device(): lax.all_gather(orbital_values, ('col', 'rep'), axis=0, tiled=True)]
    dot_general x6 -> x0, matrix products: 72.1 us -> none  [the longest x1 29.7 us: on_device(): lax.dot_general(mixed_half, columns, (((1,), (1,)), ((), ())), preferred_...]
    reshape x3 -> x1, local copies, waits for them, and re-layouts: 53.4 us -> 0.09 us  [on_device(): flat = tile_pairs.reshape(1, 2 * n_pair)]
    gather x4 -> x0, local copies, waits for them, and re-layouts: 15.4 us -> none  [the longest x1 6.19 us: mix_rows(): jnp.take(row_tiles, second_tile, axis=1)]
    unnamed x7 -> x1, local copies, waits for them, and re-layouts: 13.5 us -> 0.75 us
    all_to_all x1 -> x0, local copies, waits for them, and re-layouts: 12.2 us -> none  [on_device(): lax.all_to_all(shaped, ('col', 'rep'), split_axis=1, concat_axis=3, tiled...]
  transfers between devices with their start and end apart: 4 -> 0, of which waited for: 2 -> 0; matrix products, arithmetic and copies ran while one was open for 2% -> 0% of each run, Pallas kernels for 0% -> 0%
where the time goes in v1:
time: 274 us
  Pallas kernels  273 us (100%)
    pallas_call x1, Pallas kernels, on_device(): pl.pallas_call(functools.partial(gather_kernel, dims), out_shape=[jax.Sha...  224 us
    pallas_call x1, Pallas kernels, on_device(): pl.pallas_call(product_kernel, grid=(block_rows // rows,), out_shape=jax....  49.2 us

profile of v1, /device:TPU:0, one launch (start us, length us, event | category | flops | bytes accessed | tf_op | source)
XLA Modules:
  0.0 274.2 jit_solution(7814789098041680305)
XLA Ops:
  0.0 0.8 copy.7
  0.8 0.1 reshape.16
  0.8 0.6 pad.4.pairs
  1.4 223.6 %shard_map.46 = (bf16[4,576,2048]{2,1,0:T(8,128)(2,1)}, bf16[4,576,2048]{2,1,0:T(8,128)(2,1)}, bf16[2048,128]{1,0:T(8,128)(2,1)}, bf16[64,128,128]{2,1,0:T(8,128)(2,1)}, s32[4,8,128]{2,1,0:T(8,128)}) custom-call(bf16[4,576,512]{2,1,0:T(8,128)(2,1)} %bitcast.6, bf16[512,128]{1,0:T(8,128)(2,1)} %orb.1, bf16[16,128,128]{2,1,0:T(8,128)(2,1)} %z.1, ...), custom_call_target="tpu_custom_call" | custom-call | tf_op jit(solution)/shard_map/pallas_call | solution.py:370
  225.0 49.2 %shard_map.47 = f32[41472,128]{1,0:T(8,128)} custom-call(s32[4,8,128]{2,1,0:T(8,128)} %get-tuple-element.10.pairs, bf16[2048,128]{1,0:T(8,128)(2,1)} %get-tuple-element.11.orb, bf16[64,128,128]{2,1,0:T(8,128)(2,1)} %get-tuple-element.12.z, bf16[2304,2048]{1,0:T(8,128)(2,1)} %bitcast.4, bf16[2304,2048]{1,0:T(8,128)(2,1)} %bitcast.5), custom_call_target="tpu_custom_call" | custom-call | tf_op jit(solution)/shard_map/pallas_call | solution.py:400

commit v2 on v1

--- a/solution.py
+++ b/solution.py
@@ -14,7 +14,7 @@
 def gather_kernel(dims, basis, orb, z, pairs, a_all, cols, orb_all, z_all, pairs_all,
                   loc_sem, xs_sem, xr_sem, os_sem, or_sem, zs_sem, zo_sem, zr_sem,
                   ys_sem, yr_sem, ts_sem, to_sem, tr_sem, ps_sem, po_sem, pr_sem,
-                  ds_sem, dr_sem):
+                  ds_sem, dr_sem, in_sem, held, held_orb, held_tiles, held_pairs, held_slice):
     G, R, X, K = dims
     C = X * K
     width = basis.shape[2]
@@ -37,6 +37,16 @@
         return pltpu.make_async_remote_copy(src_ref=src, dst_ref=dst, send_sem=send, recv_sem=recv,
                                             device_id=device, device_id_type=MESH)
 
+    own_rows = z.at[:, pl.ds(pl.multiple_of(c * part, 16), part), :]
+    staged = [
+        pltpu.make_async_copy(basis, held, in_sem.at[0]),
+        pltpu.make_async_copy(orb, held_orb, in_sem.at[1]),
+        pltpu.make_async_copy(own_rows, held_tiles, in_sem.at[2]),
+        pltpu.make_async_copy(pairs, held_pairs, in_sem.at[3]),
+    ]
+    for copy in staged:
+        copy.start()
+
     others = [(dx, dk) for dx in range(X) for dk in range(K) if dx or dk]
     barrier = pltpu.get_barrier_semaphore()
     for dx, dk in others:
@@ -56,8 +66,6 @@
     def tile_rows(block):
         return z_all.at[pl.ds(block * n_pair, n_pair), pl.ds(pl.multiple_of(c * part, 16), part), :]
 
-    own_rows = z.at[:, pl.ds(pl.multiple_of(c * part, 16), part), :]
-
     def up():
         return dev(row=r + 1)
 
@@ -147,12 +155,13 @@
                 orb_to(dx, dk).start()
 
     local = [
-        pltpu.make_async_copy(basis, a_all.at[:, :, lanes(c)], loc_sem.at[0]),
-        pltpu.make_async_copy(orb, own_orb, loc_sem.at[1]),
-        pltpu.make_async_copy(own_rows, tile_rows(r), loc_sem.at[2]),
-        pltpu.make_async_copy(pairs, pairs_all.at[r], loc_sem.at[3]),
+        pltpu.make_async_copy(held, a_all.at[:, :, lanes(c)], loc_sem.at[0]),
+        pltpu.make_async_copy(held_orb, own_orb, loc_sem.at[1]),
+        pltpu.make_async_copy(held_tiles, tile_rows(r), loc_sem.at[2]),
+        pltpu.make_async_copy(held_pairs, pairs_all.at[r], loc_sem.at[3]),
     ]
-    for copy in local:
+    for before, copy in zip(staged, local):
+        before.wait()
         copy.start()
 
     for dk in range(1, K):
@@ -260,7 +269,10 @@
         spread_in(dx, dk).wait_recv()
     local[0].wait()
     local[1].wait()
-    own = pltpu.make_async_copy(a_all.at[c], cols.at[r], loc_sem.at[4])
+    take = pltpu.make_async_copy(a_all.at[c], held_slice, in_sem.at[4])
+    take.start()
+    take.wait()
+    own = pltpu.make_async_copy(held_slice, cols.at[r], loc_sem.at[4])
     own.start()
 
     def finish(block, carry):
@@ -383,9 +395,16 @@
             dma((R, C)), dma((2, C)), dma((R, C)),
             dma((G - 1, R, C)), dma((G - 1, R, C)),
             dma((R,)), dma((2,)), dma((R,)), dma((R,)), dma((2,)), dma((R,)),
-            dma((X, K)), dma((X, K)),
+            dma((X, K)), dma((X, K)), dma((5,)),
+            pltpu.VMEM((C, S, width), bf16),
+            pltpu.VMEM((width, orbs), bf16),
+            pltpu.VMEM((n_pair, tile // C, tile), bf16),
+            pltpu.VMEM((8, 128), jnp.int32),
+            pltpu.VMEM((S, points), bf16),
         ],
-        compiler_params=pltpu.CompilerParams(collective_id=0, has_side_effects=True),
+        compiler_params=pltpu.CompilerParams(
+            collective_id=0, has_side_effects=True, vmem_limit_bytes=40 * 1024 * 1024
+        ),
     )(basis_values.reshape(C, S, width), orbital_values, z_tiles, flat)
 
     a = a_all.reshape(C * S, points)

time: 274 us -> 171 us (0.62)
  Pallas kernels: 273 us -> 164 us
  local copies, waits for them, and re-layouts: 1.44 us -> 7.16 us
    pallas_call x1, Pallas kernels: 224 us -> 114 us  [on_device(): pl.pallas_call(functools.partial(gather_kernel, dims), out_shape=[jax.Sha...]
    unnamed x1 -> x13, local copies, waits for them, and re-layouts: 0.75 us -> 7.06 us
where the time goes in v2:
time: 171 us
  Pallas kernels  164 us (96%)
  local copies, waits for them, and re-layouts  7.16 us (4%)
    pallas_call x1, Pallas kernels, on_device(): pl.pallas_call(functools.partial(gather_kernel, dims), out_shape=[jax.Sha...  114 us
    pallas_call x1, Pallas kernels, on_device(): pl.pallas_call(product_kernel, grid=(block_rows // rows,), out_shape=jax....  49.2 us
    unnamed x13, local copies, waits for them, and re-layouts  7.06 us

profile of v2, /device:TPU:0, one launch (start us, length us, event | category | flops | bytes accessed | tf_op | source)
XLA Modules:
  0.0 170.7 jit_solution(2455957402084490183)
XLA Ops:
  0.0 0.8 copy.7
  0.8 0.1 reshape.16
  0.9 0.0 copy-start
  0.9 1.7 copy-done
  2.5 0.0 copy-start.3
  2.5 1.0 copy-done.3
  3.6 0.0 copy-start.4
  3.6 0.9 copy-done.4
  4.5 114.4 %shard_map.46 = (bf16[4,576,2048]{2,1,0:T(8,128)(2,1)}, bf16[4,576,2048]{2,1,0:T(8,128)(2,1)}, bf16[2048,128]{1,0:T(8,128)(2,1)S(1)}, bf16[64,128,128]{2,1,0:T(8,128)(2,1)S(1)}, s32[4,8,128]{2,1,0:T(8,128)S(1)}) custom-call(bf16[4,576,512]{2,1,0:T(8,128)(2,1)S(1)} %bitcast.4, bf16[512,128]{1,0:T(8,128)(2,1)S(1)} %copy-done.4, ...), custom_call_target="tpu_custom_call" | custom-call | tf_op jit(solution)/shard_map/pallas_call | solution.py:382
  118.9 0.0 copy-start.1
  118.9 1.3 copy-done.1
  120.2 0.0 copy-start.2
  120.2 0.8 copy-done.2
  121.0 0.0 copy-start.5
  121.0 0.6 copy-done.5
  121.6 49.2 %shard_map.47 = f32[41472,128]{1,0:T(8,128)} custom-call(s32[4,8,128]{2,1,0:T(8,128)} %copy-done.5, bf16[2048,128]{1,0:T(8,128)(2,1)} %copy-done.2, bf16[64,128,128]{2,1,0:T(8,128)(2,1)} %copy-done.1, bf16[2304,2048]{1,0:T(8,128)(2,1)} %bitcast.5, bf16[2304,2048]{1,0:T(8,128)(2,1)} %bitcast.6), custom_call_target="tpu_custom_call" | custom-call | tf_op jit(solution)/shard_map/pallas_call | solution.py:419
  (1 shorter events, 0.0 us)
Async XLA Ops:
  0.9 1.7 copy-start
  2.5 1.0 copy-start.3
  3.6 0.9 copy-start.4
  118.9 1.3 copy-start.1
  120.2 0.8 copy-start.2
  121.0 0.6 copy-start.5

commit v3 on v2

--- a/solution.py
+++ b/solution.py
@@ -145,14 +145,14 @@
         return remote(ref, ref, os_sem.at[dx, dk], or_sem.at[dx, dk], dev(dk=1))
 
     order = [(dx, dk) for dx in range(X) for dk in range(K)]
-    for ex, ek in order:
+    def send_slices(ex, ek):
         for dk in range(1, K):
             to_core(dk, lax.rem(x + ex, X) * K + lax.rem(k + K - dk + ek, K)).start()
         for dx in range(1, X):
             to_chip(dx, lax.rem(x + X - dx + ex, X) * K + lax.rem(k + ek, K)).start()
-        if ex == 0 and ek == 0:
-            for dx, dk in others:
-                orb_to(dx, dk).start()
+
+    for ek in range(K):
+        send_slices(0, ek)
 
     local = [
         pltpu.make_async_copy(held, a_all.at[:, :, lanes(c)], loc_sem.at[0]),
@@ -212,9 +212,6 @@
         ref = all_rows(col_of(dx, dk))
         return remote(ref, ref, ds_sem.at[dx, dk], dr_sem.at[dx, dk], dev(dk=1))
 
-    for dx, dk in others:
-        spread(dx, dk).start()
-
     relay(1, [0])
     for dx in range(1, X):
         from_other(dx, 0, c).wait_recv()
@@ -224,6 +221,11 @@
             s = col_of(0, K - dk)
             from_other(dx, 0, s).wait_recv()
             hand_on(dx, dk, s).start()
+    for ex in range(1, X):
+        for ek in range(K):
+            send_slices(ex, ek)
+    for dx, dk in others:
+        orb_to(dx, dk).start()
     for dx in range(1, X):
         for dk in range(1, K):
             from_other(dx, dk, c).wait_recv()
@@ -239,6 +241,9 @@
 
     lax.fori_loop(2, R, first_part, 0)
     relay(1, list(range(1, X)))
+
+    for dx, dk in others:
+        spread(dx, dk).start()
 
     for dx in range(1, X):
         for ex, ek in order:
@@ -403,7 +408,7 @@
             pltpu.VMEM((S, points), bf16),
         ],
         compiler_params=pltpu.CompilerParams(
-            collective_id=0, has_side_effects=True, vmem_limit_bytes=40 * 1024 * 1024
+            collective_id=0, has_side_effects=True, vmem_limit_bytes=60 * 1024 * 1024
         ),
     )(basis_values.reshape(C, S, width), orbital_values, z_tiles, flat)
 

time: 171 us -> 165 us (0.965)
  local copies, waits for them, and re-layouts: 7.16 us -> 1.44 us
    unnamed x13 -> x1, local copies, waits for them, and re-layouts: 7.06 us -> 0.75 us
where the time goes in v3:
time: 165 us
  Pallas kernels  164 us (99%)
    pallas_call x1, Pallas kernels, on_device(): pl.pallas_call(functools.partial(gather_kernel, dims), out_shape=[jax.Sha...  115 us
    pallas_call x1, Pallas kernels, on_device(): pl.pallas_call(product_kernel, grid=(block_rows // rows,), out_shape=jax....  49.2 us

profile of v3, /device:TPU:0, one launch (start us, length us, event | category | flops | bytes accessed | tf_op | source)
XLA Modules:
  0.0 165.3 jit_solution(12175450416419603267)
XLA Ops:
  0.0 0.8 copy.7
  0.8 0.1 reshape.16
  0.8 0.6 pad.4.pairs
  1.4 114.6 %shard_map.46 = (bf16[4,576,2048]{2,1,0:T(8,128)(2,1)}, bf16[4,576,2048]{2,1,0:T(8,128)(2,1)}, bf16[2048,128]{1,0:T(8,128)(2,1)}, bf16[64,128,128]{2,1,0:T(8,128)(2,1)}, s32[4,8,128]{2,1,0:T(8,128)}) custom-call(bf16[4,576,512]{2,1,0:T(8,128)(2,1)} %bitcast.6, bf16[512,128]{1,0:T(8,128)(2,1)} %orb.1, bf16[16,128,128]{2,1,0:T(8,128)(2,1)} %z.1, ...), custom_call_target="tpu_custom_call" | custom-call | tf_op jit(solution)/shard_map/pallas_call | solution.py:387
  116.1 49.2 %shard_map.47 = f32[41472,128]{1,0:T(8,128)} custom-call(s32[4,8,128]{2,1,0:T(8,128)} %get-tuple-element.10.pairs, bf16[2048,128]{1,0:T(8,128)(2,1)} %get-tuple-element.11.orb, bf16[64,128,128]{2,1,0:T(8,128)(2,1)} %get-tuple-element.12.z, bf16[2304,2048]{1,0:T(8,128)(2,1)} %bitcast.4, bf16[2304,2048]{1,0:T(8,128)(2,1)} %bitcast.5), custom_call_target="tpu_custom_call" | custom-call | tf_op jit(solution)/shard_map/pallas_call | solution.py:424
